TPU v7x, 256 devices: a whole 4x4x8 slice. The times are simulated.
256 devices in a mesh: dp: 64 (over z, x, core), tower: 2 (over y_hi), replica: 2 (over y_lo).
Axes of the slice: x: 4, y: 4 (y_hi: 2, y_lo: 2; y = y_hi * 2 + y_lo), z: 8, core: 2. Of those that a mesh axis runs over, the one named last changes fastest.
Arguments:
- feature_vectors: bfloat16 [2, 163840, 1152], P('tower', ('replica', 'dp')), parts along dimension 1, may hold values from -6 to 6
- sample_source_label: int32 [163840], P('replica'), parts along dimension 0, may hold values from 0 to 40959
- sharpness_factor_array: float32 [1], replicated, may hold values from 20 to 40
- logit_offset_array: float32 [1], replicated, may hold values from -3 to 0
Outputs:
- grad_embeddings: float32 [2, 163840, 1152], P('tower', ('replica', 'dp')), parts along dimension 1
There are 2 independent parts, one for each index of `replica`. A program takes and returns all parts, laid end to end along the dimension named above; an argument that names none is the same for every part. Nothing has to cross between parts.
All inputs are finite; a program needn't handle non-finite values.
Results may differ from a plain program's by a relative error of at most 0.0058.
Values may be sent and summed in bfloat16 or wider, within the bound.
No kernel may reach another device: no remote copies, remote signals or barrier semaphores. Data moves between devices by JAX's collectives and lax.ppermute only.
A program may use at most 128 MiB of HBM per device.

v0:
```python
import functools

import jax
import jax.numpy as jnp
from jax import lax
from jax.experimental import pallas as pl
from jax.experimental.pallas import tpu as pltpu
from jax.sharding import PartitionSpec as P

ROWS = 640
N_BLOCKS = 128
LANES = 128
TILE = 320
PER_BLOCK = ROWS // TILE
VMEM_LIMIT = 16 * 2**20
epsilon = 1e-06

FIRST = ((0, 256), (256, 384))
SECOND = ((0, 384), (384, 256))

VMEM = pl.BlockSpec(memory_space=pltpu.VMEM)
SMEM = pl.BlockSpec(memory_space=pltpu.SMEM)
ANY = pl.BlockSpec(memory_space=pl.ANY)

Y1, X, A, Y2, Z, B = range(6)


def moved(array, step, cores=None):
    length = lax.axis_size("dp")
    pairs = []
    for i in range(length):
        for tower, sign in ((0, 1), (1, -1)):
            if cores is None or (i % 2) ^ tower == cores:
                pairs.append((2 * i + tower, 2 * ((i + sign * step) % length) + tower))
    return lax.ppermute(array, ("dp", "tower"), pairs)


def swapped(name, array):
    with jax.named_scope(name):
        return lax.ppermute(array, "tower", [(0, 1), (1, 0)])


def onward(name, array):
    with jax.named_scope(name):
        return moved(array, 1)


def back(name, array):
    with jax.named_scope(name):
        return moved(array, -1)


def chip_onward(name, array):
    with jax.named_scope(name):
        return moved(array, 2, 0)


def core_onward(name, array):
    with jax.named_scope(name):
        return moved(array, 1, 0)


def after(array, token):
    return lax.optimization_barrier((array, token))[0]


def inverse_norm_of(rows):
    return lax.rsqrt(jnp.sum(rows * rows, axis=-1, keepdims=True) + epsilon)


def normed_rows(rows):
    rows = rows.astype(jnp.float32)
    return (rows * inverse_norm_of(rows)).astype(jnp.bfloat16)


def norm_kernel(parts, place_ref, lead_ref, features_ref, out_ref, *part_refs):
    tower, core = place_ref[0], place_ref[1]
    for tile in range(2 * PER_BLOCK):
        block, within = tile // PER_BLOCK, tile % PER_BLOCK
        start = pl.multiple_of((block ^ tower) * ROWS + within * TILE, TILE)
        out_ref[pl.ds(tile * TILE, TILE), :] = normed_rows(features_ref[0, pl.ds(start, TILE), :])
    for (second, start, size), part_ref in zip(parts, part_refs):
        block = (core if second else 1 - core) ^ tower
        part_ref[...] = out_ref[pl.ds(pl.multiple_of(block * ROWS + start, LANES), size), :]


def norm_rows(place, lead, features, parts):
    width = features.shape[-1]
    sizes = [2 * ROWS] + [n for _, _, n in parts]
    return pl.pallas_call(
        functools.partial(norm_kernel, parts),
        out_shape=[jax.ShapeDtypeStruct((n, width), jnp.bfloat16) for n in sizes],
        in_specs=[SMEM, ANY, VMEM],
        out_specs=[VMEM] * len(sizes),
        compiler_params=pltpu.CompilerParams(vmem_limit_bytes=VMEM_LIMIT),
    )(place, lead, features)


def label_kernel(blocks_ref, labels_ref, own_ref, other_ref):
    per_block = ROWS // LANES
    for slot in range(8):
        for i in range(per_block):
            line = labels_ref[pl.ds(blocks_ref[slot] * per_block + i, 1), :]
            if slot < 6:
                other_ref[slot, :, pl.ds(i * LANES, LANES)] = line
            else:
                rows = pl.ds((slot - 6) * ROWS + i * LANES, LANES)
                own_ref[rows, :] = jnp.transpose(jnp.broadcast_to(line, (LANES, LANES)))


def label_rows(blocks, labels):
    return pl.pallas_call(
        label_kernel,
        out_shape=[
            jax.ShapeDtypeStruct((2 * ROWS, LANES), jnp.int32),
            jax.ShapeDtypeStruct((6, 1, ROWS), jnp.int32),
        ],
        in_specs=[SMEM, VMEM],
        out_specs=[VMEM, VMEM],
        compiler_params=pltpu.CompilerParams(vmem_limit_bytes=VMEM_LIMIT),
    )(blocks, labels.reshape(-1, LANES))


def update_kernel(pieces, spans, raw, has_old, finish, place_ref, sharpness_ref, shift_ref, *refs):
    refs = list(refs)
    own_ref, own_label_ref, other_label_ref = refs[:3]
    del refs[:3]
    tower, role = place_ref[0], place_ref[2]
    sharpness, shift = sharpness_ref[0], shift_ref[0]
    chunk_refs = [[refs.pop(0) for _ in range(count)] for _, _, _, count in pieces]
    old_ref = refs.pop(0) if has_old else None
    if finish:
        features_ref, out_ref, others_ref, staging, sems = refs
    else:
        out_ref, others_ref = refs
    at, labels = 0, []
    for (slot, start, size, _), choices in zip(pieces, chunk_refs):
        rows = pl.ds(at, size)
        if len(choices) == 1:
            others_ref[rows, :] = choices[0][...]
        else:

            @pl.when(role == 0)
            def _():
                others_ref[rows, :] = choices[0][...]

            @pl.when(role != 0)
            def _():
                others_ref[rows, :] = choices[1][...]

        if raw:
            others_ref[rows, :] = normed_rows(others_ref[rows, :])
        labels.append(other_label_ref[slot][:, start : start + size])
        at += size
    labels = jnp.concatenate(labels, axis=1)
    copies = []
    tiles = 2 * ROWS // TILE

    def others_of(tile):
        low, high = spans[tile // PER_BLOCK]
        return others_ref[pl.ds(low, high - low), :]

    def inner_of(tile):
        own = own_ref[pl.ds(tile * TILE, TILE), :]
        return lax.dot_general(
            own, others_of(tile), (((1,), (1,)), ((), ())), preferred_element_type=jnp.float32
        )

    upcoming = inner_of(0)
    for tile in range(tiles):
        block, within = tile // PER_BLOCK, tile % PER_BLOCK
        low, high = spans[block]
        rows = pl.ds(tile * TILE, TILE)
        inner = upcoming
        if tile + 1 < tiles:
            upcoming = inner_of(tile + 1)
        logit = inner * sharpness + shift
        same = own_label_ref[rows, :1] == labels[:, low:high]
        grown = jnp.exp(jnp.where(same, logit, -logit))
        weight = (jnp.where(same, -sharpness, sharpness) / (1.0 + grown)).astype(jnp.bfloat16)
        total = jnp.dot(weight, others_of(tile), preferred_element_type=jnp.float32)
        if has_old:
            total = old_ref[rows, :] + total
        if not finish:
            out_ref[rows, :] = total
            continue
        native = pl.ds(pl.multiple_of((block ^ tower) * ROWS + within * TILE, TILE), TILE)
        raw = features_ref[0, native, :].astype(jnp.float32)
        inverse_norm = inverse_norm_of(raw)
        unit = raw * inverse_norm
        projected = jnp.sum(unit * total, axis=-1, keepdims=True)
        staging[tile] = inverse_norm * (total - unit * projected)
        copy = pltpu.make_async_copy(staging.at[tile], out_ref.at[0, native, :], sems.at[tile])
        copy.start()
        copies.append(copy)
    for copy in copies:
        copy.wait()


def update(scalars, own, own_labels, other_labels, pieces, spans, grads, raw=False, features=None):
    width = own.shape[-1]
    finish = features is not None
    chunks = [array for *_, arrays in pieces for array in arrays]
    pieces = [(slot, start, size, len(arrays)) for slot, start, size, arrays in pieces]
    operands = [*scalars, own, own_labels, other_labels, *chunks]
    if grads is not None:
        operands.append(grads)
    depth = sum(size for _, _, size, _ in pieces)
    scratch = [pltpu.VMEM((depth, width), jnp.bfloat16)]
    if finish:
        operands.append(features)
        tiles = 2 * ROWS // TILE
        scratch += [pltpu.VMEM((tiles, TILE, width), jnp.float32), pltpu.SemaphoreType.DMA((tiles,))]
    shape = (1, 2 * ROWS, width) if finish else (2 * ROWS, width)
    return pl.pallas_call(
        functools.partial(update_kernel, pieces, spans, raw, grads is not None, finish),
        out_shape=jax.ShapeDtypeStruct(shape, jnp.float32),
        in_specs=[SMEM] * len(scalars) + [VMEM] * (len(operands) - len(scalars)),
        out_specs=ANY if finish else VMEM,
        scratch_shapes=scratch,
        compiler_params=pltpu.CompilerParams(vmem_limit_bytes=VMEM_LIMIT),
        cost_estimate=pl.CostEstimate(flops=1, bytes_accessed=1, transcendentals=0),
    )(*operands)


def per_device(feature_vectors, sample_source_label, sharpness_factor_array, logit_offset_array):
    tower = lax.axis_index("tower")
    dp = lax.axis_index("dp")
    core = dp % 2
    role = core ^ tower
    place = jnp.stack([tower, core, role]).astype(jnp.int32)

    a0, a1 = (n for _, n in FIRST)
    b0, b1 = (n for _, n in SECOND)
    lead = lax.dynamic_slice_in_dim(feature_vectors[0], (1 - core) * ROWS, a0)
    parts = [(False, *FIRST[1]), (True, *SECOND[0]), (True, *SECOND[1])]
    normed, part, *early = norm_rows(place, lead, feature_vectors, parts)

    def block_at(index):
        chip = 4 * (dp // 2)
        return jnp.where(tower == 0, chip + index, chip + 3 - index) % N_BLOCKS

    held = [1 + role, 3 * role - 2, 5 * role - 3, role - 1, 3 * role, -role, 2 * role, 2 * role + 1]
    blocks = jnp.stack([block_at(index) for index in held]).astype(jnp.int32)
    own_labels, other_labels = label_rows(blocks, sample_source_label)
    scalars = (place, sharpness_factor_array, logit_offset_array)
    run = functools.partial(update, scalars, normed, own_labels, other_labels)

    y0 = swapped("y0", lead)
    y1 = swapped("y1", part)
    y0 = after(y0, normed)
    e0, e1 = back("e0", early[0]), back("e1", after(early[1], y0))
    y2 = swapped("y2", e0)
    x0, w0 = onward("x0", y0), chip_onward("w0", y0)

    cut0, cut1 = FIRST
    cut2, cut3 = SECOND
    grads = run(
        [(A, *cut0, (w0, y0)), (X, *cut0, (x0,)), (Y1, *cut0, (y0,))], ((0, 2 * a0), (a0, 3 * a0)), None, raw=True
    )
    y1 = after(y1, x0)
    x1, w1 = onward("x1", y1), chip_onward("w1", y1)
    y2 = after(y2, grads)
    y3 = swapped("y3", after(e1, grads))
    z2, c2 = back("z2", y2), core_onward("c2", y2)
    pieces = [(X, *cut1, (x1,)), (Y2, *cut2, (y2,)), (Y1, *cut1, (y1,))]
    grads = run(pieces, ((0, a1 + b0), (0, 2 * a1 + b0)), grads)
    y3 = after(y3, grads)
    z3, c3 = back("z3", y3), core_onward("c3", y3)
    pieces = [(A, *cut1, (w1, y1)), (B, *cut2, (z2, c2)), (Y2, *cut3, (y3,)), (Z, *cut2, (z2,))]
    grads = run(pieces, ((0, a1 + b0 + b1), (a1 + b0, a1 + 2 * b0 + b1)), grads)
    pieces = [(B, *cut3, (z3, c3)), (Z, *cut3, (z3,))]
    return run(pieces, ((0, b1), (b1, 2 * b1)), grads, features=feature_vectors)


def solution(mesh):
    placed = (P("tower", ("replica", "dp"), None), P("replica"), P(), P())
    return jax.shard_map(
        per_device,
        mesh=mesh,
        in_specs=placed,
        out_specs=P("tower", ("replica", "dp"), None),
        check_vma=False,
    )
```

profile of v0, /device:TPU:8, one launch (start us, length us, event | category | flops | bytes accessed | tf_op | source)
XLA Modules:
  0.0 92.1 jit_solution(8656718955894381641)
XLA Ops:
  0.0 1.9 %dynamic-slice_bitcast_fusion.lead_ref = bf16[256,1152]{1,0:T(8,128)(2,1)} fusion(bf16[1,1280,1152]{2,1,0:T(8,128)(2,1)} %refs_7_.1, s32[]{:T(128)S(6)} %select_n.78), kind=kLoop, calls=%fused_computation | loop fusion | bytes 1179652 | tf_op jit(solution)/shard_map/dynamic_slice | solution.py:235
  1.9 2.3 %collective-permute-start = (bf16[256,1152]{1,0:T(8,128)(2,1)}, bf16[256,1152]{1,0:T(8,128)(2,1)S(1)}, u32[]{:S(2)}, u32[]{:S(2)}) collective-permute-start(bf16[256,1152]{1,0:T(8,128)(2,1)} %dynamic-slice_bitcast_fusion.lead_ref), channel_id=1, source_target_pairs={{0,2},{2,0},{1,3},{3,1},{4,6},{6,4},{5,7},{7,5},{8,10},{10,8},{9,1... | collective-permute-start | bytes 1769480 | tf_op jit(solution)/shard_map/y0/ppermute | solution.py:40
  4.2 0.1 pad_add_fusion.place_ref
  4.3 0.0 copy-start
  4.3 1.8 %copy-done = bf16[1,1280,1152]{2,1,0:T(8,128)(2,1)S(1)} copy-done((bf16[1,1280,1152]{2,1,0:T(8,128)(2,1)S(1)}, bf16[1,1280,1152]{2,1,0:T(8,128)(2,1)}, u32[]{:S(2)}) %copy-start) | copy-done | bytes 2949144
  6.1 2.5 %shard_map.46 = (bf16[1280,1152]{1,0:T(8,128)(2,1)S(1)}, bf16[384,1152]{1,0:T(8,128)(2,1)S(1)}, bf16[384,1152]{1,0:T(8,128)(2,1)S(1)}, bf16[256,1152]{1,0:T(8,128)(2,1)}) custom-call(s32[3]{0:T(128)S(1)} %pad_add_fusion.place_ref, bf16[256,1152]{1,0:T(8,128)(2,1)} %dynamic-slice_bitcast_fusion.lead_ref, bf16[1,1280,1152]{2,1,0:T(8,128)(2,1)S(1)} %copy-done), custom_call_target="tpu_custom_call" | custom-call | tf_op jit(solution)/shard_map/pallas_call | solution.py:90
  8.6 7.2 %collective-permute-start.7 = (bf16[384,1152]{1,0:T(8,128)(2,1)S(1)}, bf16[384,1152]{1,0:T(8,128)(2,1)}, u32[]{:S(2)}, u32[]{:S(2)}) collective-permute-start(bf16[384,1152]{1,0:T(8,128)(2,1)S(1)} %get-tuple-element.26), channel_id=1, source_target_pairs={{0,252},{2,6},{4,0},{6,10},{8,4},{10,14},{12,8},{14,18},{16,12},{1... | collective-permute-start | bytes 2654216 | tf_op jit(solution)/shard_map/e0/ppermute | solution.py:35
  15.8 0.0 collective-permute-start.5
  15.8 4.0 %collective-permute-done.refs_4_.refs_6_ = bf16[256,1152]{1,0:T(8,128)(2,1)S(1)} collective-permute-done((bf16[256,1152]{1,0:T(8,128)(2,1)}, bf16[256,1152]{1,0:T(8,128)(2,1)S(1)}, u32[]{:S(2)}, u32[]{:S(2)}) %collective-permute-start) | collective-permute-done | bytes 589856 | tf_op jit(solution)/shard_map/y0/ppermute | solution.py:40
  19.9 0.0 collective-permute-start.3
  19.9 3.4 %collective-permute-start.2 = (bf16[256,1152]{1,0:T(8,128)(2,1)S(1)}, bf16[256,1152]{1,0:T(8,128)(2,1)}, u32[]{:S(2)}, u32[]{:S(2)}) collective-permute-start(bf16[256,1152]{1,0:T(8,128)(2,1)S(1)} %collective-permute-done.refs_4_.refs_6_), channel_id=1, source_target_pairs={{0,8},{6,254},{8,16},{14,6},{16,24},{22,14},{24,32},{30,22},{32,40... | collective-permute-start | bytes 1769480 | tf_op jit(solution)/shard_map/w0/ppermute | solution.py:35
  23.3 3.6 %collective-permute-start.1 = (bf16[256,1152]{1,0:T(8,128)(2,1)}, bf16[256,1152]{1,0:T(8,128)(2,1)}, u32[]{:S(2)}, u32[]{:S(2)}) collective-permute-start(bf16[256,1152]{1,0:T(8,128)(2,1)} %get-tuple-element.22), channel_id=1, source_target_pairs={{0,252},{2,6},{4,0},{6,10},{8,4},{10,14},{12,8},{14,18},{16,12},{1... | collective-permute-start | bytes 1769480 | tf_op jit(solution)/shard_map/e1/ppermute | solution.py:35
  26.8 0.0 collective-permute-done.7
  26.8 5.6 %collective-permute-start.8 = (bf16[384,1152]{1,0:T(8,128)(2,1)}, bf16[384,1152]{1,0:T(8,128)(2,1)}, u32[]{:S(2)}, u32[]{:S(2)}) collective-permute-start(bf16[384,1152]{1,0:T(8,128)(2,1)} %collective-permute-done.7), channel_id=1, source_target_pairs={{0,2},{2,0},{1,3},{3,1},{4,6},{6,4},{5,7},{7,5},{8,10},{10,8},{9,1... | collective-permute-start | bytes 2654216 | tf_op jit(solution)/shard_map/y2/ppermute | solution.py:40
  32.4 7.6 %collective-permute-done.5.refs_5_.refs_4_ = bf16[384,1152]{1,0:T(8,128)(2,1)} collective-permute-done((bf16[384,1152]{1,0:T(8,128)(2,1)S(1)}, bf16[384,1152]{1,0:T(8,128)(2,1)}, u32[]{:S(2)}, u32[]{:S(2)}) %collective-permute-start.5) | collective-permute-done | bytes 884768 | tf_op jit(solution)/shard_map/y1/ppermute | solution.py:40
  40.0 0.0 collective-permute-done.3.refs_5_
  40.0 0.0 copy-start.2
  40.0 0.8 copy-done.2
  40.8 0.0 collective-permute-start.6
  42.2 0.1 stack.51.blocks_ref
  42.3 0.0 copy-start.4
  42.3 1.0 %copy-done.4 = s32[81920]{0:T(1024)S(1)} copy-done((s32[81920]{0:T(1024)S(1)}, s32[81920]{0:T(1024)}, u32[]{:S(2)}) %copy-start.4) | copy-done | bytes 327704
  43.2 0.8 shard_map.47
  44.0 0.0 collective-permute-done.2.refs_3_
  44.0 0.0 copy-start.3
  44.0 1.1 %copy-done.3 = bf16[256,1152]{1,0:T(8,128)(2,1)S(1)} copy-done((bf16[256,1152]{1,0:T(8,128)(2,1)S(1)}, bf16[256,1152]{1,0:T(8,128)(2,1)}, u32[]{:S(2)}) %copy-start.3) | copy-done | bytes 589848
  45.1 5.3 %shard_map.48.refs_6_ = f32[1280,1152]{1,0:T(8,128)S(1)} custom-call(s32[3]{0:T(128)S(1)} %pad_add_fusion.place_ref, f32[1]{0:T(128)S(6)} %copy.5.sharpness_ref, f32[1]{0:T(128)S(6)} %copy.6.shift_ref, bf16[1280,1152]{1,0:T(8,128)(2,1)S(1)} %get-tuple-element.17.refs_0_, s32[1280,128]{1,0:T(8,128)S(1)} %get-tuple-element.18.refs_1_, ...), custom_call_target="tpu_custom_call" | custom-call | flops 1 | bytes 1 | tf_op jit(solution)/shard_map/pallas_call | solution.py:215
  50.4 0.0 collective-permute-done.1
  50.4 6.8 %collective-permute-start.4 = (bf16[256,1152]{1,0:T(8,128)(2,1)}, bf16[256,1152]{1,0:T(8,128)(2,1)S(1)}, u32[]{:S(2)}, u32[]{:S(2)}) collective-permute-start(bf16[256,1152]{1,0:T(8,128)(2,1)} %collective-permute-done.1), channel_id=1, source_target_pairs={{0,2},{2,0},{1,3},{3,1},{4,6},{6,4},{5,7},{7,5},{8,10},{10,8},{9,1... | collective-permute-start | bytes 1769480 | tf_op jit(solution)/shard_map/y3/ppermute | solution.py:40
  57.1 1.9 %collective-permute-start.11 = (bf16[384,1152]{1,0:T(8,128)(2,1)}, bf16[384,1152]{1,0:T(8,128)(2,1)S(1)}, u32[]{:S(2)}, u32[]{:S(2)}) collective-permute-start(bf16[384,1152]{1,0:T(8,128)(2,1)} %collective-permute-done.5.refs_5_.refs_4_), channel_id=1, source_target_pairs={{0,8},{6,254},{8,16},{14,6},{16,24},{22,14},{24,32},{30,22},{32,40... | collective-permute-start | bytes 2654216 | tf_op jit(solution)/shard_map/w1/ppermute | solution.py:35
  59.0 0.0 collective-permute-done.8.refs_4_
  59.1 4.3 %collective-permute-start.12 = (bf16[384,1152]{1,0:T(8,128)(2,1)}, bf16[384,1152]{1,0:T(8,128)(2,1)S(1)}, u32[]{:S(2)}, u32[]{:S(2)}) collective-permute-start(bf16[384,1152]{1,0:T(8,128)(2,1)} %collective-permute-done.8.refs_4_), channel_id=1, source_target_pairs={{0,252},{2,6},{4,0},{6,10},{8,4},{10,14},{12,8},{14,18},{16,12},{1... | collective-permute-start | bytes 2654216 | tf_op jit(solution)/shard_map/z2/ppermute | solution.py:35
  63.4 1.5 %collective-permute-start.13 = (bf16[384,1152]{1,0:T(8,128)(2,1)}, bf16[384,1152]{1,0:T(8,128)(2,1)S(1)}, u32[]{:S(2)}, u32[]{:S(2)}) collective-permute-start(bf16[384,1152]{1,0:T(8,128)(2,1)} %collective-permute-done.8.refs_4_), channel_id=1, source_target_pairs={{0,4},{6,2},{8,12},{14,10},{16,20},{22,18},{24,28},{30,26},{32,36}... | collective-permute-start | bytes 2654216 | tf_op jit(solution)/shard_map/c2/ppermute | solution.py:35
  64.9 0.0 collective-permute-done.6.refs_3_
  64.9 8.9 %shard_map.49.refs_9_ = f32[1280,1152]{1,0:T(8,128)S(1)} custom-call(s32[3]{0:T(128)S(1)} %pad_add_fusion.place_ref, f32[1]{0:T(128)S(6)} %copy.5.sharpness_ref, f32[1]{0:T(128)S(6)} %copy.6.shift_ref, bf16[1280,1152]{1,0:T(8,128)(2,1)S(1)} %get-tuple-element.17.refs_0_, s32[1280,128]{1,0:T(8,128)S(1)} %get-tuple-element.18.refs_1_, ...), custom_call_target="tpu_custom_call" | custom-call | flops 1 | bytes 1 | tf_op jit(solution)/shard_map/pallas_call | solution.py:215
  73.8 0.0 copy-start.1
  73.8 0.0 collective-permute-done.4.refs_7_
  73.9 1.6 %collective-permute-start.10 = (bf16[256,1152]{1,0:T(8,128)(2,1)S(1)}, bf16[256,1152]{1,0:T(8,128)(2,1)S(1)}, u32[]{:S(2)}, u32[]{:S(2)}) collective-permute-start(bf16[256,1152]{1,0:T(8,128)(2,1)S(1)} %collective-permute-done.4.refs_7_), channel_id=1, source_target_pairs={{0,4},{6,2},{8,12},{14,10},{16,20},{22,18},{24,28},{30,26},{32,36}... | collective-permute-start | bytes 1769480 | tf_op jit(solution)/shard_map/c3/ppermute | solution.py:35
  75.5 2.7 %collective-permute-start.9 = (bf16[256,1152]{1,0:T(8,128)(2,1)S(1)}, bf16[256,1152]{1,0:T(8,128)(2,1)S(1)}, u32[]{:S(2)}, u32[]{:S(2)}) collective-permute-start(bf16[256,1152]{1,0:T(8,128)(2,1)S(1)} %collective-permute-done.4.refs_7_), channel_id=1, source_target_pairs={{0,252},{2,6},{4,0},{6,10},{8,4},{10,14},{12,8},{14,18},{16,12},{1... | collective-permute-start | bytes 1769480 | tf_op jit(solution)/shard_map/z3/ppermute | solution.py:35
  78.1 0.0 collective-permute-done.11.refs_3_
  78.1 0.0 collective-permute-done.12.refs_5_.refs_8_
  78.1 0.0 collective-permute-done.13.refs_6_
  78.1 7.9 %shard_map.50.refs_6_ = f32[1280,1152]{1,0:T(8,128)S(1)} custom-call(s32[3]{0:T(128)S(1)} %pad_add_fusion.place_ref, f32[1]{0:T(128)S(6)} %copy.5.sharpness_ref, f32[1]{0:T(128)S(6)} %copy.6.shift_ref, bf16[1280,1152]{1,0:T(8,128)(2,1)S(1)} %get-tuple-element.17.refs_0_, s32[1280,128]{1,0:T(8,128)S(1)} %get-tuple-element.18.refs_1_, ...), custom_call_target="tpu_custom_call" | custom-call | flops 1 | bytes 1 | tf_op jit(solution)/shard_map/pallas_call | solution.py:215
  86.0 0.0 collective-permute-done.10.refs_4_
  86.0 0.0 collective-permute-done.9.refs_3_.refs_5_
  86.1 0.0 copy-done.1
  86.1 5.9 %shard_map.51 = f32[1,1280,1152]{2,1,0:T(8,128)} custom-call(s32[3]{0:T(128)S(1)} %pad_add_fusion.place_ref, f32[1]{0:T(128)S(6)} %copy.5.sharpness_ref, f32[1]{0:T(128)S(6)} %copy.6.shift_ref, bf16[1280,1152]{1,0:T(8,128)(2,1)S(1)} %get-tuple-element.17.refs_0_, s32[1280,128]{1,0:T(8,128)S(1)} %get-tuple-element.18.refs_1_, ...), custom_call_target="tpu_custom_call" | custom-call | flops 1 | bytes 1 | tf_op jit(solution)/shard_map/pallas_call | solution.py:215
Async XLA Ops:
  1.9 17.9 %collective-permute-start = (bf16[256,1152]{1,0:T(8,128)(2,1)}, bf16[256,1152]{1,0:T(8,128)(2,1)S(1)}, u32[]{:S(2)}, u32[]{:S(2)}) collective-permute-start(bf16[256,1152]{1,0:T(8,128)(2,1)} %dynamic-slice_bitcast_fusion.lead_ref), channel_id=1, source_target_pairs={{0,2},{2,0},{1,3},{3,1},{4,6},{6,4},{5,7},{7,5},{8,10},{10,8},{9,1... | collective-permute-start | bytes 1769480 | tf_op jit(solution)/shard_map/y0/ppermute | solution.py:40
  4.3 1.8 %copy-start = (bf16[1,1280,1152]{2,1,0:T(8,128)(2,1)S(1)}, bf16[1,1280,1152]{2,1,0:T(8,128)(2,1)}, u32[]{:S(2)}) copy-start(bf16[1,1280,1152]{2,1,0:T(8,128)(2,1)} %refs_7_.1) | copy-start | bytes 8847364
  8.6 18.2 %collective-permute-start.7 = (bf16[384,1152]{1,0:T(8,128)(2,1)S(1)}, bf16[384,1152]{1,0:T(8,128)(2,1)}, u32[]{:S(2)}, u32[]{:S(2)}) collective-permute-start(bf16[384,1152]{1,0:T(8,128)(2,1)S(1)} %get-tuple-element.26), channel_id=1, source_target_pairs={{0,252},{2,6},{4,0},{6,10},{8,4},{10,14},{12,8},{14,18},{16,12},{1... | collective-permute-start | bytes 2654216 | tf_op jit(solution)/shard_map/e0/ppermute | solution.py:35
  15.8 24.2 %collective-permute-start.5 = (bf16[384,1152]{1,0:T(8,128)(2,1)S(1)}, bf16[384,1152]{1,0:T(8,128)(2,1)}, u32[]{:S(2)}, u32[]{:S(2)}) collective-permute-start(bf16[384,1152]{1,0:T(8,128)(2,1)S(1)} %get-tuple-element.24), channel_id=1, source_target_pairs={{0,2},{2,0},{1,3},{3,1},{4,6},{6,4},{5,7},{7,5},{8,10},{10,8},{9,1... | collective-permute-start | bytes 2654216 | tf_op jit(solution)/shard_map/y1/ppermute | solution.py:40
  19.9 20.2 %collective-permute-start.3 = (bf16[256,1152]{1,0:T(8,128)(2,1)S(1)}, bf16[256,1152]{1,0:T(8,128)(2,1)S(1)}, u32[]{:S(2)}, u32[]{:S(2)}) collective-permute-start(bf16[256,1152]{1,0:T(8,128)(2,1)S(1)} %collective-permute-done.refs_4_.refs_6_), channel_id=1, source_target_pairs={{0,4},{2,254},{4,8},{6,2},{8,12},{10,6},{12,16},{14,10},{16,20},{1... | collective-permute-start | bytes 1769480 | tf_op jit(solution)/shard_map/x0/ppermute | solution.py:35
  19.9 24.2 %collective-permute-start.2 = (bf16[256,1152]{1,0:T(8,128)(2,1)S(1)}, bf16[256,1152]{1,0:T(8,128)(2,1)}, u32[]{:S(2)}, u32[]{:S(2)}) collective-permute-start(bf16[256,1152]{1,0:T(8,128)(2,1)S(1)} %collective-permute-done.refs_4_.refs_6_), channel_id=1, source_target_pairs={{0,8},{6,254},{8,16},{14,6},{16,24},{22,14},{24,32},{30,22},{32,40... | collective-permute-start | bytes 1769480 | tf_op jit(solution)/shard_map/w0/ppermute | solution.py:35
  23.3 27.1 %collective-permute-start.1 = (bf16[256,1152]{1,0:T(8,128)(2,1)}, bf16[256,1152]{1,0:T(8,128)(2,1)}, u32[]{:S(2)}, u32[]{:S(2)}) collective-permute-start(bf16[256,1152]{1,0:T(8,128)(2,1)} %get-tuple-element.22), channel_id=1, source_target_pairs={{0,252},{2,6},{4,0},{6,10},{8,4},{10,14},{12,8},{14,18},{16,12},{1... | collective-permute-start | bytes 1769480 | tf_op jit(solution)/shard_map/e1/ppermute | solution.py:35
  26.8 32.2 %collective-permute-start.8 = (bf16[384,1152]{1,0:T(8,128)(2,1)}, bf16[384,1152]{1,0:T(8,128)(2,1)}, u32[]{:S(2)}, u32[]{:S(2)}) collective-permute-start(bf16[384,1152]{1,0:T(8,128)(2,1)} %collective-permute-done.7), channel_id=1, source_target_pairs={{0,2},{2,0},{1,3},{3,1},{4,6},{6,4},{5,7},{7,5},{8,10},{10,8},{9,1... | collective-permute-start | bytes 2654216 | tf_op jit(solution)/shard_map/y2/ppermute | solution.py:40
  40.0 0.8 copy-start.2
  40.8 24.0 %collective-permute-start.6 = (bf16[384,1152]{1,0:T(8,128)(2,1)}, bf16[384,1152]{1,0:T(8,128)(2,1)}, u32[]{:S(2)}, u32[]{:S(2)}) collective-permute-start(bf16[384,1152]{1,0:T(8,128)(2,1)} %collective-permute-done.5.refs_5_.refs_4_), channel_id=1, source_target_pairs={{0,4},{2,254},{4,8},{6,2},{8,12},{10,6},{12,16},{14,10},{16,20},{1... | collective-permute-start | bytes 2654216 | tf_op jit(solution)/shard_map/x1/ppermute | solution.py:35
  42.3 1.0 %copy-start.4 = (s32[81920]{0:T(1024)S(1)}, s32[81920]{0:T(1024)}, u32[]{:S(2)}) copy-start(s32[81920]{0:T(1024)} %param.5) | copy-start | bytes 983044
  44.0 1.1 %copy-start.3 = (bf16[256,1152]{1,0:T(8,128)(2,1)S(1)}, bf16[256,1152]{1,0:T(8,128)(2,1)}, u32[]{:S(2)}) copy-start(bf16[256,1152]{1,0:T(8,128)(2,1)} %copy-done.2) | copy-start | bytes 1769476
  50.4 23.5 %collective-permute-start.4 = (bf16[256,1152]{1,0:T(8,128)(2,1)}, bf16[256,1152]{1,0:T(8,128)(2,1)S(1)}, u32[]{:S(2)}, u32[]{:S(2)}) collective-permute-start(bf16[256,1152]{1,0:T(8,128)(2,1)} %collective-permute-done.1), channel_id=1, source_target_pairs={{0,2},{2,0},{1,3},{3,1},{4,6},{6,4},{5,7},{7,5},{8,10},{10,8},{9,1... | collective-permute-start | bytes 1769480 | tf_op jit(solution)/shard_map/y3/ppermute | solution.py:40
  57.1 21.0 %collective-permute-start.11 = (bf16[384,1152]{1,0:T(8,128)(2,1)}, bf16[384,1152]{1,0:T(8,128)(2,1)S(1)}, u32[]{:S(2)}, u32[]{:S(2)}) collective-permute-start(bf16[384,1152]{1,0:T(8,128)(2,1)} %collective-permute-done.5.refs_5_.refs_4_), channel_id=1, source_target_pairs={{0,8},{6,254},{8,16},{14,6},{16,24},{22,14},{24,32},{30,22},{32,40... | collective-permute-start | bytes 2654216 | tf_op jit(solution)/shard_map/w1/ppermute | solution.py:35
  59.1 19.1 %collective-permute-start.12 = (bf16[384,1152]{1,0:T(8,128)(2,1)}, bf16[384,1152]{1,0:T(8,128)(2,1)S(1)}, u32[]{:S(2)}, u32[]{:S(2)}) collective-permute-start(bf16[384,1152]{1,0:T(8,128)(2,1)} %collective-permute-done.8.refs_4_), channel_id=1, source_target_pairs={{0,252},{2,6},{4,0},{6,10},{8,4},{10,14},{12,8},{14,18},{16,12},{1... | collective-permute-start | bytes 2654216 | tf_op jit(solution)/shard_map/z2/ppermute | solution.py:35
  63.4 14.8 %collective-permute-start.13 = (bf16[384,1152]{1,0:T(8,128)(2,1)}, bf16[384,1152]{1,0:T(8,128)(2,1)S(1)}, u32[]{:S(2)}, u32[]{:S(2)}) collective-permute-start(bf16[384,1152]{1,0:T(8,128)(2,1)} %collective-permute-done.8.refs_4_), channel_id=1, source_target_pairs={{0,4},{6,2},{8,12},{14,10},{16,20},{22,18},{24,28},{30,26},{32,36}... | collective-permute-start | bytes 2654216 | tf_op jit(solution)/shard_map/c2/ppermute | solution.py:35
  73.8 12.2 %copy-start.1 = (bf16[1,1280,1152]{2,1,0:T(8,128)(2,1)S(1)}, bf16[1,1280,1152]{2,1,0:T(8,128)(2,1)}, u32[]{:S(2)}) copy-start(bf16[1,1280,1152]{2,1,0:T(8,128)(2,1)} %refs_7_.1) | copy-start | bytes 8847364
  73.9 12.2 %collective-permute-start.10 = (bf16[256,1152]{1,0:T(8,128)(2,1)S(1)}, bf16[256,1152]{1,0:T(8,128)(2,1)S(1)}, u32[]{:S(2)}, u32[]{:S(2)}) collective-permute-start(bf16[256,1152]{1,0:T(8,128)(2,1)S(1)} %collective-permute-done.4.refs_7_), channel_id=1, source_target_pairs={{0,4},{6,2},{8,12},{14,10},{16,20},{22,18},{24,28},{30,26},{32,36}... | collective-permute-start | bytes 1769480 | tf_op jit(solution)/shard_map/c3/ppermute | solution.py:35
  75.5 10.6 %collective-permute-start.9 = (bf16[256,1152]{1,0:T(8,128)(2,1)S(1)}, bf16[256,1152]{1,0:T(8,128)(2,1)S(1)}, u32[]{:S(2)}, u32[]{:S(2)}) collective-permute-start(bf16[256,1152]{1,0:T(8,128)(2,1)S(1)} %collective-permute-done.4.refs_7_), channel_id=1, source_target_pairs={{0,252},{2,6},{4,0},{6,10},{8,4},{10,14},{12,8},{14,18},{16,12},{1... | collective-permute-start | bytes 1769480 | tf_op jit(solution)/shard_map/z3/ppermute | solution.py:35
where the time goes:
time: 93.6 us; the launch traced here: 92.1 us
  starting transfers between devices  40.8 us (44%)
  Pallas kernels  31.2 us (33%)
  waiting for transfers between devices  11.7 us (12%)
  local copies, waits for them, and re-layouts  6.7 us (7%)
  between operations  1.68 us (2%)
    pallas_call x4, Pallas kernels, update(): pl.pallas_call(functools.partial(update_kernel, pieces, spans, raw, grads...  28 us
    ppermute x10, starting transfers between devices, moved(): return lax.ppermute(array, ('dp', 'tower'), pairs)  26.2 us
    ppermute x4, starting transfers between devices, swapped(): return lax.ppermute(array, 'tower', [(0, 1), (1, 0)])  14.6 us
    ppermute x4, waiting for transfers between devices, swapped(): return lax.ppermute(array, 'tower', [(0, 1), (1, 0)])  11.6 us
    unnamed x10, local copies, waits for them, and re-layouts  4.69 us
    pallas_call x1, Pallas kernels, norm_rows(): pl.pallas_call(functools.partial(norm_kernel, parts), out_shape=[jax.Shap...  2.48 us
    dynamic_slice x1, local copies, waits for them, and re-layouts, per_device(): lead = lax.dynamic_slice_in_dim(feature_vectors[0], (1 - core) * ROWS, a0)  1.92 us
  transfers between devices with their start and end apart: 14, of which 2 were waited for; matrix products, arithmetic and copies ran while one was open for 0% of the time, Pallas kernels for 27%

commit v1 on v0

--- a/solution.py
+++ b/solution.py
@@ -71,6 +71,24 @@
 def normed_rows(rows):
     rows = rows.astype(jnp.float32)
     return (rows * inverse_norm_of(rows)).astype(jnp.bfloat16)
+
+
+def lead_kernel(features_ref, out_ref, sem):
+    start = pl.multiple_of((1 - lax.axis_index("dp") % 2) * ROWS, ROWS)
+    copy = pltpu.make_async_copy(features_ref.at[0, pl.ds(start, out_ref.shape[0]), :], out_ref, sem)
+    copy.start()
+    copy.wait()
+
+
+def lead_rows(features, count):
+    return pl.pallas_call(
+        lead_kernel,
+        out_shape=jax.ShapeDtypeStruct((count, features.shape[-1]), features.dtype),
+        in_specs=[ANY],
+        out_specs=VMEM,
+        scratch_shapes=[pltpu.SemaphoreType.DMA],
+        compiler_params=pltpu.CompilerParams(vmem_limit_bytes=60 * 2**20),
+    )(features)
 
 
 def norm_kernel(parts, place_ref, lead_ref, features_ref, out_ref, *part_refs):
@@ -134,7 +152,7 @@
     else:
         out_ref, others_ref = refs
     at, labels = 0, []
-    for (slot, start, size, _), choices in zip(pieces, chunk_refs):
+    for index, ((slot, start, size, _), choices) in enumerate(zip(pieces, chunk_refs)):
         rows = pl.ds(at, size)
         if len(choices) == 1:
             others_ref[rows, :] = choices[0][...]
@@ -148,7 +166,7 @@
             def _():
                 others_ref[rows, :] = choices[1][...]
 
-        if raw:
+        if index < raw:
             others_ref[rows, :] = normed_rows(others_ref[rows, :])
         labels.append(other_label_ref[slot][:, start : start + size])
         at += size
@@ -197,7 +215,7 @@
         copy.wait()
 
 
-def update(scalars, own, own_labels, other_labels, pieces, spans, grads, raw=False, features=None):
+def update(scalars, own, own_labels, other_labels, pieces, spans, grads, raw=0, features=None):
     width = own.shape[-1]
     finish = features is not None
     chunks = [array for *_, arrays in pieces for array in arrays]
@@ -232,7 +250,7 @@
 
     a0, a1 = (n for _, n in FIRST)
     b0, b1 = (n for _, n in SECOND)
-    lead = lax.dynamic_slice_in_dim(feature_vectors[0], (1 - core) * ROWS, a0)
+    lead = lead_rows(feature_vectors, a0)
     parts = [(False, *FIRST[1]), (True, *SECOND[0]), (True, *SECOND[1])]
     normed, part, *early = norm_rows(place, lead, feature_vectors, parts)
 
@@ -248,27 +266,26 @@
 
     y0 = swapped("y0", lead)
     y1 = swapped("y1", part)
-    y0 = after(y0, normed)
+    y0 = after(y0, (normed, own_labels, other_labels))
     e0, e1 = back("e0", early[0]), back("e1", after(early[1], y0))
     y2 = swapped("y2", e0)
     x0, w0 = onward("x0", y0), chip_onward("w0", y0)
 
     cut0, cut1 = FIRST
     cut2, cut3 = SECOND
-    grads = run(
-        [(A, *cut0, (w0, y0)), (X, *cut0, (x0,)), (Y1, *cut0, (y0,))], ((0, 2 * a0), (a0, 3 * a0)), None, raw=True
-    )
     y1 = after(y1, x0)
     x1, w1 = onward("x1", y1), chip_onward("w1", y1)
+    pieces = [(A, *cut0, (w0, y0)), (X, *cut0, (x0,)), (Y1, *cut0, (y0,)), (Y1, *cut1, (y1,))]
+    grads = run(pieces, ((0, 2 * a0), (a0, 3 * a0 + a1)), None, raw=3)
     y2 = after(y2, grads)
-    y3 = swapped("y3", after(e1, grads))
+    y3 = swapped("y3", e1)
     z2, c2 = back("z2", y2), core_onward("c2", y2)
-    pieces = [(X, *cut1, (x1,)), (Y2, *cut2, (y2,)), (Y1, *cut1, (y1,))]
-    grads = run(pieces, ((0, a1 + b0), (0, 2 * a1 + b0)), grads)
+    grads = run([(X, *cut1, (x1,)), (Y2, *cut2, (y2,))], ((0, a1 + b0), (0, a1 + b0)), grads)
     y3 = after(y3, grads)
     z3, c3 = back("z3", y3), core_onward("c3", y3)
     pieces = [(A, *cut1, (w1, y1)), (B, *cut2, (z2, c2)), (Y2, *cut3, (y3,)), (Z, *cut2, (z2,))]
     grads = run(pieces, ((0, a1 + b0 + b1), (a1 + b0, a1 + 2 * b0 + b1)), grads)
+    z3 = after(z3, grads)
     pieces = [(B, *cut3, (z3, c3)), (Z, *cut3, (z3,))]
     return run(pieces, ((0, b1), (b1, 2 * b1)), grads, features=feature_vectors)
 

time: 93.6 us -> 91.8 us (0.981); the launches traced: 92.1 us -> 91.3 us
  starting transfers between devices: 40.8 us -> 32.8 us
  waiting for transfers between devices: 11.7 us -> 19.4 us
  local copies, waits for them, and re-layouts: 6.7 us -> 4.8 us
  Pallas kernels: 31.2 us -> 32.6 us
    ppermute x10, waiting for transfers between devices: 0.03 us -> 8.96 us  [moved(): return lax.ppermute(array, ('dp', 'tower'), pairs)]
    ppermute x4, starting transfers between devices: 14.6 us -> 8.01 us  [swapped(): return lax.ppermute(array, 'tower', [(0, 1), (1, 0)])]
    dynamic_slice x1 -> x0, local copies, waits for them, and re-layouts: 1.92 us -> none  [per_device(): lead = lax.dynamic_slice_in_dim(feature_vectors[0], (1 - core) * ROWS, a0)]
    pallas_call x0 -> x1, Pallas kernels: none -> 1.89 us  [lead_rows(): pl.pallas_call(lead_kernel, out_shape=jax.ShapeDtypeStruct((count, featur...]
    ppermute x10, starting transfers between devices: 26.2 us -> 24.8 us  [moved(): return lax.ppermute(array, ('dp', 'tower'), pairs)]
    ppermute x4, waiting for transfers between devices: 11.6 us -> 10.5 us  [swapped(): return lax.ppermute(array, 'tower', [(0, 1), (1, 0)])]
  transfers between devices with their start and end apart: 14 -> 14, of which waited for: 2 -> 3; matrix products, arithmetic and copies ran while one was open for 0% -> 0% of each run, Pallas kernels for 27% -> 27%
where the time goes in v1:
time: 91.8 us; the launch traced here: 91.3 us
  starting transfers between devices  32.8 us (36%)
  Pallas kernels  32.6 us (36%)
  waiting for transfers between devices  19.4 us (21%)
  local copies, waits for them, and re-layouts  4.8 us (5%)
  between operations  1.66 us (2%)
    pallas_call x4, Pallas kernels, update(): pl.pallas_call(functools.partial(update_kernel, pieces, spans, raw, grads...  27.1 us
    ppermute x10, starting transfers between devices, moved(): return lax.ppermute(array, ('dp', 'tower'), pairs)  24.8 us
    ppermute x4, waiting for transfers between devices, swapped(): return lax.ppermute(array, 'tower', [(0, 1), (1, 0)])  10.5 us
    ppermute x10, waiting for transfers between devices, moved(): return lax.ppermute(array, ('dp', 'tower'), pairs)  8.96 us
    ppermute x4, starting transfers between devices, swapped(): return lax.ppermute(array, 'tower', [(0, 1), (1, 0)])  8.01 us
    unnamed x10, local copies, waits for them, and re-layouts  4.71 us
    pallas_call x1, Pallas kernels, norm_rows(): pl.pallas_call(functools.partial(norm_kernel, parts), out_shape=[jax.Shap...  2.8 us
    pallas_call x1, Pallas kernels, lead_rows(): pl.pallas_call(lead_kernel, out_shape=jax.ShapeDtypeStruct((count, featur...  1.89 us
  transfers between devices with their start and end apart: 14, of which 3 were waited for; matrix products, arithmetic and copies ran while one was open for 0% of the time, Pallas kernels for 27%

profile of v1, /device:TPU:8, one launch (start us, length us, event | category | flops | bytes accessed | tf_op | source)
XLA Modules:
  0.0 91.3 jit_solution(15334086564255215913)
XLA Ops:
  0.0 1.9 %shard_map.46.lead_ref = bf16[256,1152]{1,0:T(8,128)(2,1)} custom-call(bf16[1,1280,1152]{2,1,0:T(8,128)(2,1)} %refs_7_.1), custom_call_target="tpu_custom_call" | custom-call | tf_op jit(solution)/shard_map/pallas_call | solution.py:84
  1.9 2.4 %collective-permute-start = (bf16[256,1152]{1,0:T(8,128)(2,1)}, bf16[256,1152]{1,0:T(8,128)(2,1)S(1)}, u32[]{:S(2)}, u32[]{:S(2)}) collective-permute-start(bf16[256,1152]{1,0:T(8,128)(2,1)} %shard_map.46.lead_ref), channel_id=1, source_target_pairs={{0,2},{2,0},{1,3},{3,1},{4,6},{6,4},{5,7},{7,5},{8,10},{10,8},{9,1... | collective-permute-start | bytes 1769480 | tf_op jit(solution)/shard_map/y0/ppermute | solution.py:40
  4.3 0.1 pad_add_fusion.place_ref
  4.4 0.0 copy-start
  4.4 1.8 %copy-done = bf16[1,1280,1152]{2,1,0:T(8,128)(2,1)S(1)} copy-done((bf16[1,1280,1152]{2,1,0:T(8,128)(2,1)S(1)}, bf16[1,1280,1152]{2,1,0:T(8,128)(2,1)}, u32[]{:S(2)}) %copy-start) | copy-done | bytes 2949144
  6.2 0.0 copy-start.2
  6.2 1.1 %copy-done.2 = bf16[256,1152]{1,0:T(8,128)(2,1)S(1)} copy-done((bf16[256,1152]{1,0:T(8,128)(2,1)S(1)}, bf16[256,1152]{1,0:T(8,128)(2,1)}, u32[]{:S(2)}) %copy-start.2) | copy-done | bytes 589848
  7.3 2.8 %shard_map.47 = (bf16[1280,1152]{1,0:T(8,128)(2,1)S(1)}, bf16[384,1152]{1,0:T(8,128)(2,1)}, bf16[384,1152]{1,0:T(8,128)(2,1)}, bf16[256,1152]{1,0:T(8,128)(2,1)S(1)}) custom-call(s32[3]{0:T(128)S(1)} %pad_add_fusion.place_ref, bf16[256,1152]{1,0:T(8,128)(2,1)S(1)} %copy-done.2, bf16[1,1280,1152]{2,1,0:T(8,128)(2,1)S(1)} %copy-done), custom_call_target="tpu_custom_call" | custom-call | tf_op jit(solution)/shard_map/pallas_call | solution.py:108
  10.1 0.0 copy-start.4
  10.1 0.8 copy-done.4
  10.9 7.2 %collective-permute-start.6 = (bf16[384,1152]{1,0:T(8,128)(2,1)}, bf16[384,1152]{1,0:T(8,128)(2,1)}, u32[]{:S(2)}, u32[]{:S(2)}) collective-permute-start(bf16[384,1152]{1,0:T(8,128)(2,1)} %get-tuple-element.25), channel_id=1, source_target_pairs={{0,252},{2,6},{4,0},{6,10},{8,4},{10,14},{12,8},{14,18},{16,12},{1... | collective-permute-start | bytes 2654216 | tf_op jit(solution)/shard_map/e0/ppermute | solution.py:35
  18.1 0.0 collective-permute-start.3
  18.1 0.1 stack.51.blocks_ref
  18.2 0.0 copy-start.3
  18.2 1.0 %copy-done.3 = s32[81920]{0:T(1024)S(1)} copy-done((s32[81920]{0:T(1024)S(1)}, s32[81920]{0:T(1024)}, u32[]{:S(2)}) %copy-start.3) | copy-done | bytes 327704
  19.2 0.8 shard_map.48
  19.9 0.0 collective-permute-done.refs_4_.refs_6_
  20.0 0.1 collective-permute-start.4
  20.0 8.9 %collective-permute-done.6 = bf16[384,1152]{1,0:T(8,128)(2,1)} collective-permute-done((bf16[384,1152]{1,0:T(8,128)(2,1)}, bf16[384,1152]{1,0:T(8,128)(2,1)}, u32[]{:S(2)}, u32[]{:S(2)}) %collective-permute-start.6) | collective-permute-done | bytes 884768 | tf_op jit(solution)/shard_map/e0/ppermute | solution.py:35
  29.0 1.4 %collective-permute-start.7 = (bf16[384,1152]{1,0:T(8,128)(2,1)}, bf16[384,1152]{1,0:T(8,128)(2,1)S(1)}, u32[]{:S(2)}, u32[]{:S(2)}) collective-permute-start(bf16[384,1152]{1,0:T(8,128)(2,1)} %collective-permute-done.6), channel_id=1, source_target_pairs={{0,2},{2,0},{1,3},{3,1},{4,6},{6,4},{5,7},{7,5},{8,10},{10,8},{9,1... | collective-permute-start | bytes 2654216 | tf_op jit(solution)/shard_map/y2/ppermute | solution.py:40
  30.4 3.8 %collective-permute-start.1 = (bf16[256,1152]{1,0:T(8,128)(2,1)}, bf16[256,1152]{1,0:T(8,128)(2,1)S(1)}, u32[]{:S(2)}, u32[]{:S(2)}) collective-permute-start(bf16[256,1152]{1,0:T(8,128)(2,1)} %copy-done.4), channel_id=1, source_target_pairs={{0,252},{2,6},{4,0},{6,10},{8,4},{10,14},{12,8},{14,18},{16,12},{1... | collective-permute-start | bytes 1769480 | tf_op jit(solution)/shard_map/e1/ppermute | solution.py:35
  34.2 1.9 %collective-permute-start.8 = (bf16[256,1152]{1,0:T(8,128)(2,1)S(1)}, bf16[256,1152]{1,0:T(8,128)(2,1)S(1)}, u32[]{:S(2)}, u32[]{:S(2)}) collective-permute-start(bf16[256,1152]{1,0:T(8,128)(2,1)S(1)} %collective-permute-done.refs_4_.refs_6_), channel_id=1, source_target_pairs={{0,8},{6,254},{8,16},{14,6},{16,24},{22,14},{24,32},{30,22},{32,40... | collective-permute-start | bytes 1769480 | tf_op jit(solution)/shard_map/w0/ppermute | solution.py:35
  36.1 6.4 %collective-permute-done.3.refs_7_.refs_4_ = bf16[384,1152]{1,0:T(8,128)(2,1)} collective-permute-done((bf16[384,1152]{1,0:T(8,128)(2,1)}, bf16[384,1152]{1,0:T(8,128)(2,1)}, u32[]{:S(2)}, u32[]{:S(2)}) %collective-permute-start.3) | collective-permute-done | bytes 884768 | tf_op jit(solution)/shard_map/y1/ppermute | solution.py:40
  42.5 0.0 collective-permute-done.4.refs_5_
  42.5 0.0 collective-permute-start.5
  42.5 0.0 collective-permute-done.1
  42.5 4.2 %collective-permute-start.2 = (bf16[256,1152]{1,0:T(8,128)(2,1)S(1)}, bf16[256,1152]{1,0:T(8,128)(2,1)S(1)}, u32[]{:S(2)}, u32[]{:S(2)}) collective-permute-start(bf16[256,1152]{1,0:T(8,128)(2,1)S(1)} %collective-permute-done.1), channel_id=1, source_target_pairs={{0,2},{2,0},{1,3},{3,1},{4,6},{6,4},{5,7},{7,5},{8,10},{10,8},{9,1... | collective-permute-start | bytes 1769480 | tf_op jit(solution)/shard_map/y3/ppermute | solution.py:40
  48.1 1.9 %collective-permute-start.10 = (bf16[384,1152]{1,0:T(8,128)(2,1)}, bf16[384,1152]{1,0:T(8,128)(2,1)S(1)}, u32[]{:S(2)}, u32[]{:S(2)}) collective-permute-start(bf16[384,1152]{1,0:T(8,128)(2,1)} %collective-permute-done.3.refs_7_.refs_4_), channel_id=1, source_target_pairs={{0,8},{6,254},{8,16},{14,6},{16,24},{22,14},{24,32},{30,22},{32,40... | collective-permute-start | bytes 2654216 | tf_op jit(solution)/shard_map/w1/ppermute | solution.py:35
  50.0 0.0 collective-permute-done.8.refs_3_
  50.0 7.3 %shard_map.49.refs_5_ = f32[1280,1152]{1,0:T(8,128)S(1)} custom-call(s32[3]{0:T(128)S(1)} %pad_add_fusion.place_ref, f32[1]{0:T(128)S(6)} %copy.5.sharpness_ref, f32[1]{0:T(128)S(6)} %copy.6.shift_ref, bf16[1280,1152]{1,0:T(8,128)(2,1)S(1)} %get-tuple-element.17.refs_0_, s32[1280,128]{1,0:T(8,128)S(1)} %get-tuple-element.18.refs_1_, ...), custom_call_target="tpu_custom_call" | custom-call | flops 1 | bytes 1 | tf_op jit(solution)/shard_map/pallas_call | solution.py:233
  57.3 4.1 %collective-permute-done.7.refs_4_ = bf16[384,1152]{1,0:T(8,128)(2,1)S(1)} collective-permute-done((bf16[384,1152]{1,0:T(8,128)(2,1)}, bf16[384,1152]{1,0:T(8,128)(2,1)S(1)}, u32[]{:S(2)}, u32[]{:S(2)}) %collective-permute-start.7) | collective-permute-done | bytes 884768 | tf_op jit(solution)/shard_map/y2/ppermute | solution.py:40
  61.4 1.9 %collective-permute-start.11 = (bf16[384,1152]{1,0:T(8,128)(2,1)S(1)}, bf16[384,1152]{1,0:T(8,128)(2,1)S(1)}, u32[]{:S(2)}, u32[]{:S(2)}) collective-permute-start(bf16[384,1152]{1,0:T(8,128)(2,1)S(1)} %collective-permute-done.7.refs_4_), channel_id=1, source_target_pairs={{0,252},{2,6},{4,0},{6,10},{8,4},{10,14},{12,8},{14,18},{16,12},{1... | collective-permute-start | bytes 2654216 | tf_op jit(solution)/shard_map/z2/ppermute | solution.py:35
  63.3 1.3 %collective-permute-start.12 = (bf16[384,1152]{1,0:T(8,128)(2,1)S(1)}, bf16[384,1152]{1,0:T(8,128)(2,1)S(1)}, u32[]{:S(2)}, u32[]{:S(2)}) collective-permute-start(bf16[384,1152]{1,0:T(8,128)(2,1)S(1)} %collective-permute-done.7.refs_4_), channel_id=1, source_target_pairs={{0,4},{6,2},{8,12},{14,10},{16,20},{22,18},{24,28},{30,26},{32,36}... | collective-permute-start | bytes 2654216 | tf_op jit(solution)/shard_map/c2/ppermute | solution.py:35
  64.6 0.0 collective-permute-done.5.refs_3_
  64.7 6.3 %shard_map.50.refs_9_ = f32[1280,1152]{1,0:T(8,128)S(1)} custom-call(s32[3]{0:T(128)S(1)} %pad_add_fusion.place_ref, f32[1]{0:T(128)S(6)} %copy.5.sharpness_ref, f32[1]{0:T(128)S(6)} %copy.6.shift_ref, bf16[1280,1152]{1,0:T(8,128)(2,1)S(1)} %get-tuple-element.17.refs_0_, s32[1280,128]{1,0:T(8,128)S(1)} %get-tuple-element.18.refs_1_, ...), custom_call_target="tpu_custom_call" | custom-call | flops 1 | bytes 1 | tf_op jit(solution)/shard_map/pallas_call | solution.py:233
  70.9 0.0 copy-start.1
  70.9 0.0 collective-permute-done.2.refs_7_
  71.0 5.0 %collective-permute-start.9 = (bf16[256,1152]{1,0:T(8,128)(2,1)S(1)}, bf16[256,1152]{1,0:T(8,128)(2,1)S(1)}, u32[]{:S(2)}, u32[]{:S(2)}) collective-permute-start(bf16[256,1152]{1,0:T(8,128)(2,1)S(1)} %collective-permute-done.2.refs_7_), channel_id=1, source_target_pairs={{0,252},{2,6},{4,0},{6,10},{8,4},{10,14},{12,8},{14,18},{16,12},{1... | collective-permute-start | bytes 1769480 | tf_op jit(solution)/shard_map/z3/ppermute | solution.py:35
  75.9 1.5 %collective-permute-start.13 = (bf16[256,1152]{1,0:T(8,128)(2,1)S(1)}, bf16[256,1152]{1,0:T(8,128)(2,1)S(1)}, u32[]{:S(2)}, u32[]{:S(2)}) collective-permute-start(bf16[256,1152]{1,0:T(8,128)(2,1)S(1)} %collective-permute-done.2.refs_7_), channel_id=1, source_target_pairs={{0,4},{6,2},{8,12},{14,10},{16,20},{22,18},{24,28},{30,26},{32,36}... | collective-permute-start | bytes 1769480 | tf_op jit(solution)/shard_map/c3/ppermute | solution.py:35
  77.5 0.0 collective-permute-done.10.refs_3_
  77.5 0.0 collective-permute-done.11.refs_5_.refs_8_
  77.5 0.0 collective-permute-done.12.refs_6_
  77.5 7.7 %shard_map.51.refs_6_ = f32[1280,1152]{1,0:T(8,128)S(1)} custom-call(s32[3]{0:T(128)S(1)} %pad_add_fusion.place_ref, f32[1]{0:T(128)S(6)} %copy.5.sharpness_ref, f32[1]{0:T(128)S(6)} %copy.6.shift_ref, bf16[1280,1152]{1,0:T(8,128)(2,1)S(1)} %get-tuple-element.17.refs_0_, s32[1280,128]{1,0:T(8,128)S(1)} %get-tuple-element.18.refs_1_, ...), custom_call_target="tpu_custom_call" | custom-call | flops 1 | bytes 1 | tf_op jit(solution)/shard_map/pallas_call | solution.py:233
  85.2 0.0 collective-permute-done.9.refs_3_.refs_5_
  85.2 0.0 collective-permute-done.13.refs_4_
  85.2 0.0 copy-done.1
  85.2 5.9 %shard_map.52 = f32[1,1280,1152]{2,1,0:T(8,128)} custom-call(s32[3]{0:T(128)S(1)} %pad_add_fusion.place_ref, f32[1]{0:T(128)S(6)} %copy.5.sharpness_ref, f32[1]{0:T(128)S(6)} %copy.6.shift_ref, bf16[1280,1152]{1,0:T(8,128)(2,1)S(1)} %get-tuple-element.17.refs_0_, s32[1280,128]{1,0:T(8,128)S(1)} %get-tuple-element.18.refs_1_, ...), custom_call_target="tpu_custom_call" | custom-call | flops 1 | bytes 1 | tf_op jit(solution)/shard_map/pallas_call | solution.py:233
Async XLA Ops:
  1.9 18.1 %collective-permute-start = (bf16[256,1152]{1,0:T(8,128)(2,1)}, bf16[256,1152]{1,0:T(8,128)(2,1)S(1)}, u32[]{:S(2)}, u32[]{:S(2)}) collective-permute-start(bf16[256,1152]{1,0:T(8,128)(2,1)} %shard_map.46.lead_ref), channel_id=1, source_target_pairs={{0,2},{2,0},{1,3},{3,1},{4,6},{6,4},{5,7},{7,5},{8,10},{10,8},{9,1... | collective-permute-start | bytes 1769480 | tf_op jit(solution)/shard_map/y0/ppermute | solution.py:40
  4.4 1.8 %copy-start = (bf16[1,1280,1152]{2,1,0:T(8,128)(2,1)S(1)}, bf16[1,1280,1152]{2,1,0:T(8,128)(2,1)}, u32[]{:S(2)}) copy-start(bf16[1,1280,1152]{2,1,0:T(8,128)(2,1)} %refs_7_.1) | copy-start | bytes 8847364
  6.2 1.1 %copy-start.2 = (bf16[256,1152]{1,0:T(8,128)(2,1)S(1)}, bf16[256,1152]{1,0:T(8,128)(2,1)}, u32[]{:S(2)}) copy-start(bf16[256,1152]{1,0:T(8,128)(2,1)} %shard_map.46.lead_ref) | copy-start | bytes 1769476
  10.1 0.8 copy-start.4
  10.9 18.1 %collective-permute-start.6 = (bf16[384,1152]{1,0:T(8,128)(2,1)}, bf16[384,1152]{1,0:T(8,128)(2,1)}, u32[]{:S(2)}, u32[]{:S(2)}) collective-permute-start(bf16[384,1152]{1,0:T(8,128)(2,1)} %get-tuple-element.25), channel_id=1, source_target_pairs={{0,252},{2,6},{4,0},{6,10},{8,4},{10,14},{12,8},{14,18},{16,12},{1... | collective-permute-start | bytes 2654216 | tf_op jit(solution)/shard_map/e0/ppermute | solution.py:35
  18.1 24.4 %collective-permute-start.3 = (bf16[384,1152]{1,0:T(8,128)(2,1)}, bf16[384,1152]{1,0:T(8,128)(2,1)}, u32[]{:S(2)}, u32[]{:S(2)}) collective-permute-start(bf16[384,1152]{1,0:T(8,128)(2,1)} %get-tuple-element.23), channel_id=1, source_target_pairs={{0,2},{2,0},{1,3},{3,1},{4,6},{6,4},{5,7},{7,5},{8,10},{10,8},{9,1... | collective-permute-start | bytes 2654216 | tf_op jit(solution)/shard_map/y1/ppermute | solution.py:40
  18.2 1.0 %copy-start.3 = (s32[81920]{0:T(1024)S(1)}, s32[81920]{0:T(1024)}, u32[]{:S(2)}) copy-start(s32[81920]{0:T(1024)} %param.5) | copy-start | bytes 983044
  20.0 22.6 %collective-permute-start.4 = (bf16[256,1152]{1,0:T(8,128)(2,1)S(1)}, bf16[256,1152]{1,0:T(8,128)(2,1)S(1)}, u32[]{:S(2)}, u32[]{:S(2)}) collective-permute-start(bf16[256,1152]{1,0:T(8,128)(2,1)S(1)} %collective-permute-done.refs_4_.refs_6_), channel_id=1, source_target_pairs={{0,4},{2,254},{4,8},{6,2},{8,12},{10,6},{12,16},{14,10},{16,20},{1... | collective-permute-start | bytes 1769480 | tf_op jit(solution)/shard_map/x0/ppermute | solution.py:35
  29.0 32.4 %collective-permute-start.7 = (bf16[384,1152]{1,0:T(8,128)(2,1)}, bf16[384,1152]{1,0:T(8,128)(2,1)S(1)}, u32[]{:S(2)}, u32[]{:S(2)}) collective-permute-start(bf16[384,1152]{1,0:T(8,128)(2,1)} %collective-permute-done.6), channel_id=1, source_target_pairs={{0,2},{2,0},{1,3},{3,1},{4,6},{6,4},{5,7},{7,5},{8,10},{10,8},{9,1... | collective-permute-start | bytes 2654216 | tf_op jit(solution)/shard_map/y2/ppermute | solution.py:40
  30.4 12.1 %collective-permute-start.1 = (bf16[256,1152]{1,0:T(8,128)(2,1)}, bf16[256,1152]{1,0:T(8,128)(2,1)S(1)}, u32[]{:S(2)}, u32[]{:S(2)}) collective-permute-start(bf16[256,1152]{1,0:T(8,128)(2,1)} %copy-done.4), channel_id=1, source_target_pairs={{0,252},{2,6},{4,0},{6,10},{8,4},{10,14},{12,8},{14,18},{16,12},{1... | collective-permute-start | bytes 1769480 | tf_op jit(solution)/shard_map/e1/ppermute | solution.py:35
  34.2 15.8 %collective-permute-start.8 = (bf16[256,1152]{1,0:T(8,128)(2,1)S(1)}, bf16[256,1152]{1,0:T(8,128)(2,1)S(1)}, u32[]{:S(2)}, u32[]{:S(2)}) collective-permute-start(bf16[256,1152]{1,0:T(8,128)(2,1)S(1)} %collective-permute-done.refs_4_.refs_6_), channel_id=1, source_target_pairs={{0,8},{6,254},{8,16},{14,6},{16,24},{22,14},{24,32},{30,22},{32,40... | collective-permute-start | bytes 1769480 | tf_op jit(solution)/shard_map/w0/ppermute | solution.py:35
  42.5 22.1 %collective-permute-start.5 = (bf16[384,1152]{1,0:T(8,128)(2,1)}, bf16[384,1152]{1,0:T(8,128)(2,1)S(1)}, u32[]{:S(2)}, u32[]{:S(2)}) collective-permute-start(bf16[384,1152]{1,0:T(8,128)(2,1)} %collective-permute-done.3.refs_7_.refs_4_), channel_id=1, source_target_pairs={{0,4},{2,254},{4,8},{6,2},{8,12},{10,6},{12,16},{14,10},{16,20},{1... | collective-permute-start | bytes 2654216 | tf_op jit(solution)/shard_map/x1/ppermute | solution.py:35
  42.5 28.4 %collective-permute-start.2 = (bf16[256,1152]{1,0:T(8,128)(2,1)S(1)}, bf16[256,1152]{1,0:T(8,128)(2,1)S(1)}, u32[]{:S(2)}, u32[]{:S(2)}) collective-permute-start(bf16[256,1152]{1,0:T(8,128)(2,1)S(1)} %collective-permute-done.1), channel_id=1, source_target_pairs={{0,2},{2,0},{1,3},{3,1},{4,6},{6,4},{5,7},{7,5},{8,10},{10,8},{9,1... | collective-permute-start | bytes 1769480 | tf_op jit(solution)/shard_map/y3/ppermute | solution.py:40
  48.1 29.4 %collective-permute-start.10 = (bf16[384,1152]{1,0:T(8,128)(2,1)}, bf16[384,1152]{1,0:T(8,128)(2,1)S(1)}, u32[]{:S(2)}, u32[]{:S(2)}) collective-permute-start(bf16[384,1152]{1,0:T(8,128)(2,1)} %collective-permute-done.3.refs_7_.refs_4_), channel_id=1, source_target_pairs={{0,8},{6,254},{8,16},{14,6},{16,24},{22,14},{24,32},{30,22},{32,40... | collective-permute-start | bytes 2654216 | tf_op jit(solution)/shard_map/w1/ppermute | solution.py:35
  61.4 16.1 %collective-permute-start.11 = (bf16[384,1152]{1,0:T(8,128)(2,1)S(1)}, bf16[384,1152]{1,0:T(8,128)(2,1)S(1)}, u32[]{:S(2)}, u32[]{:S(2)}) collective-permute-start(bf16[384,1152]{1,0:T(8,128)(2,1)S(1)} %collective-permute-done.7.refs_4_), channel_id=1, source_target_pairs={{0,252},{2,6},{4,0},{6,10},{8,4},{10,14},{12,8},{14,18},{16,12},{1... | collective-permute-start | bytes 2654216 | tf_op jit(solution)/shard_map/z2/ppermute | solution.py:35
  63.3 14.2 %collective-permute-start.12 = (bf16[384,1152]{1,0:T(8,128)(2,1)S(1)}, bf16[384,1152]{1,0:T(8,128)(2,1)S(1)}, u32[]{:S(2)}, u32[]{:S(2)}) collective-permute-start(bf16[384,1152]{1,0:T(8,128)(2,1)S(1)} %collective-permute-done.7.refs_4_), channel_id=1, source_target_pairs={{0,4},{6,2},{8,12},{14,10},{16,20},{22,18},{24,28},{30,26},{32,36}... | collective-permute-start | bytes 2654216 | tf_op jit(solution)/shard_map/c2/ppermute | solution.py:35
  70.9 14.3 %copy-start.1 = (bf16[1,1280,1152]{2,1,0:T(8,128)(2,1)S(1)}, bf16[1,1280,1152]{2,1,0:T(8,128)(2,1)}, u32[]{:S(2)}) copy-start(bf16[1,1280,1152]{2,1,0:T(8,128)(2,1)} %refs_7_.1) | copy-start | bytes 8847364
  71.0 14.3 %collective-permute-start.9 = (bf16[256,1152]{1,0:T(8,128)(2,1)S(1)}, bf16[256,1152]{1,0:T(8,128)(2,1)S(1)}, u32[]{:S(2)}, u32[]{:S(2)}) collective-permute-start(bf16[256,1152]{1,0:T(8,128)(2,1)S(1)} %collective-permute-done.2.refs_7_), channel_id=1, source_target_pairs={{0,252},{2,6},{4,0},{6,10},{8,4},{10,14},{12,8},{14,18},{16,12},{1... | collective-permute-start | bytes 1769480 | tf_op jit(solution)/shard_map/z3/ppermute | solution.py:35
  75.9 9.3 %collective-permute-start.13 = (bf16[256,1152]{1,0:T(8,128)(2,1)S(1)}, bf16[256,1152]{1,0:T(8,128)(2,1)S(1)}, u32[]{:S(2)}, u32[]{:S(2)}) collective-permute-start(bf16[256,1152]{1,0:T(8,128)(2,1)S(1)} %collective-permute-done.2.refs_7_), channel_id=1, source_target_pairs={{0,4},{6,2},{8,12},{14,10},{16,20},{22,18},{24,28},{30,26},{32,36}... | collective-permute-start | bytes 1769480 | tf_op jit(solution)/shard_map/c3/ppermute | solution.py:35
